TPU v7x, 256 devices: a whole 4x4x8 slice. The times are simulated.
256 devices in a mesh: tm: 8 (over y, core), mp: 4 (over z_lo), tok: 8 (over z_hi, x).
Axes of the slice: x: 4, y: 4, z: 8 (z_hi: 2, z_lo: 4; z = z_hi * 4 + z_lo), core: 2. Of those that a mesh axis runs over, the one named last changes fastest.
Arguments:
- features: bfloat16 [1024, 3584], P('tok'), may hold values from -6 to 6
- spike_mask: int32 [8, 1024, 3584], P('tm', 'tok'), may hold values 0 or 1
- gate_weight: bfloat16 [3584, 7168], P(('tm', 'tok'), 'mp'), may hold values from -0.09375 to 0.09375
- threshold: float32 [7168], P('mp'), may hold values from 0.5 to 2
Outputs:
- rates: float32 [1024, 7168], P('tok', 'mp')
- grad_threshold: float32 [7168], P('mp')
All inputs are finite; a program needn't handle non-finite values. No bound on the sum of `spike_mask` on one device may be relied on, other than what follows from the above.
Results may differ from a plain program's by a relative error of at most 0.00035.
Values may be sent and summed in bfloat16 or wider, within the bound.
No kernel may reach another device: no remote copies, remote signals or barrier semaphores. Data moves between devices by JAX's collectives and lax.ppermute only.
A program may use at most 64 MiB of HBM per device.

v0:
```python
import jax
import jax.numpy as jnp
from jax import lax
from jax.sharding import PartitionSpec as P

SHARP = 2.0


def passed_along(x, axis, by):
    peers = lax.axis_size(axis)
    pairs = [(i, i + by) for i in range(peers) if 0 <= i + by < peers]
    return lax.ppermute(x, axis, pairs)


def on_device(features, spike_mask, gate_weight, threshold):
    steps = lax.axis_size("tm")
    step_index = lax.axis_index("tm")
    tokens_all = features.shape[0] * lax.axis_size("tok")
    rows = features.shape[0]
    width = gate_weight.shape[1]
    driven = jnp.where(spike_mask[0] > 0, features, jnp.zeros_like(features))
    piece = lax.all_gather(gate_weight, ("tm", "tok"), axis=0, tiled=True)
    student = jnp.dot(driven, piece, preferred_element_type=jnp.float32)
    teacher = jnp.dot(features, piece, preferred_element_type=jnp.float32)
    current = 2.0 * student
    target = jax.nn.silu(teacher)
    blocks = 1
    size = rows // blocks
    turns = steps + blocks - 1

    def forward_turn(turn, carry):
        incoming, spikes = carry
        block = turn - step_index
        active = (block >= 0) & (block < blocks)
        rising = incoming + current
        fired = jax.nn.sigmoid(SHARP * (rising - threshold))
        leaving = rising - threshold * fired
        older = spikes
        spikes = jnp.where(active, fired, older)
        passed = passed_along(leaving, "tm", 1)
        return (passed, spikes)

    block_zero = jnp.zeros((size, width), jnp.float32)
    unused, spikes = lax.fori_loop(
        0, turns, forward_turn, (block_zero, jnp.zeros((rows, width), jnp.float32))
    )
    total = lax.psum(spikes, "tm")
    rates = threshold * total / steps
    error = (rates - target) / tokens_all

    def backward_turn(turn, carry):
        incoming, grad_sum = carry
        block = turn - (steps - 1 - step_index)
        active = (block >= 0) & (block < blocks)
        dspike = error * threshold / steps - threshold * incoming
        dwide = dspike * SHARP * spikes * (1.0 - spikes)
        term = jnp.sum(-dwide - spikes * incoming + error * spikes / steps, axis=0)
        grad_sum = grad_sum + jnp.where(active, term, jnp.zeros_like(term))
        passed = passed_along((incoming + dwide).astype(jnp.bfloat16), "tm", -1).astype(jnp.float32)
        return (passed, grad_sum)

    unused_cot, grad_local = lax.fori_loop(
        0, turns, backward_turn, (block_zero, jnp.zeros((width,), jnp.float32))
    )
    grad_threshold = lax.psum(grad_local, ("tm", "tok"))
    return (rates, grad_threshold)


def solution(mesh):
    return jax.shard_map(
        on_device,
        mesh=mesh,
        in_specs=(P("tok", None), P("tm", "tok", None), P(("tm", "tok"), "mp"), P("mp")),
        out_specs=(P("tok", "mp"), P("mp")),
        check_vma=False,
    )
```

profile of v0, /device:TPU:32, one launch (start us, length us, event | category | flops | bytes accessed | tf_op | source)
XLA Modules:
  0.0 676.2 jit_solution(10581541776726929995)
XLA Ops:
  8.0 140.1 %all-gather.2.cloned.1.call-done = bf16[3584,1792]{1,0:T(8,128)(2,1)} async-done(((bf16[56,1792]{1,0:T(8,128)(2,1)}), bf16[3584,1792]{1,0:T(8,128)(2,1)}) %all-gather.2.cloned.1.call-update) | async-done | bytes 12845072 | tf_op jit(solution)/shard_map/all_gather | solution.py:22
  148.0 7.4 %convolution_multiply_fusion = f32[128,1792]{1,0:T(8,128)S(1)} fusion(bf16[3584,1792]{1,0:T(8,128)(2,1)} %all-gather.2.cloned.1.call-done, bf16[128,3584]{1,0:T(8,128)(2,1)} %param.8, s32[1,128,3584]{2,1,0:T(8,128)} %param.9), kind=kOutput, calls=%fused_computation.8 | convolution fusion | flops 1645314048 | bytes 16515072 | tf_op jit(solution)/shard_map/dot_general | solution.py:23
  155.5 120.2 %while.34 = (s32[]{:T(128)}, f32[128,1792]{1,0:T(8,128)S(1)}, f32[128,1792]{1,0:T(8,128)S(1)}, f32[128,1792]{1,0:T(8,128)S(1)}, f32[1792]{0:T(1024)S(1)}, /*index=5*/s32[]{:T(128)}, s32[]{:T(128)}, s32[]{:T(128)}) while((s32[]{:T(128)}, f32[128,1792]{1,0:T(8,128)S(1)}, f32[128,1792]{1,0:T(8,128)S(1)}, f32[128,1792]{1,0:T(8,128)S(1)}, ...), condition=%wide.region_1.2_spmd.clone, body=%wide.region_0.1_spmd.clone.sunk | while | flops 2293767 | bytes 8264873 | solution.py:44
  163.1 11.6 %collective-permute-start = (f32[128,1792]{1,0:T(8,128)}, f32[128,1792]{1,0:T(8,128)S(1)}, u32[]{:S(2)}, u32[]{:S(2)}) collective-permute-start(f32[128,1792]{1,0:T(8,128)} %get-tuple-element.455), channel_id=1, source_target_pairs={{0,32},{32,64},{64,96},{96,128},{128,160},{160,192},{192,224},{1,3... | collective-permute-start | bytes 2752520 | tf_op jit(solution)/shard_map/while/body/eval_jaxpr/ppermute | solution.py:12
  178.4 12.7 %collective-permute-start = (f32[128,1792]{1,0:T(8,128)}, f32[128,1792]{1,0:T(8,128)S(1)}, u32[]{:S(2)}, u32[]{:S(2)}) collective-permute-start(f32[128,1792]{1,0:T(8,128)} %get-tuple-element.455), channel_id=1, source_target_pairs={{0,32},{32,64},{64,96},{96,128},{128,160},{160,192},{192,224},{1,3... | collective-permute-start | bytes 2752520 | tf_op jit(solution)/shard_map/while/body/eval_jaxpr/ppermute | solution.py:12
  194.9 12.7 %collective-permute-start = (f32[128,1792]{1,0:T(8,128)}, f32[128,1792]{1,0:T(8,128)S(1)}, u32[]{:S(2)}, u32[]{:S(2)}) collective-permute-start(f32[128,1792]{1,0:T(8,128)} %get-tuple-element.455), channel_id=1, source_target_pairs={{0,32},{32,64},{64,96},{96,128},{128,160},{160,192},{192,224},{1,3... | collective-permute-start | bytes 2752520 | tf_op jit(solution)/shard_map/while/body/eval_jaxpr/ppermute | solution.py:12
  207.6 2.2 collective-permute-done
  211.4 12.7 %collective-permute-start = (f32[128,1792]{1,0:T(8,128)}, f32[128,1792]{1,0:T(8,128)S(1)}, u32[]{:S(2)}, u32[]{:S(2)}) collective-permute-start(f32[128,1792]{1,0:T(8,128)} %get-tuple-element.455), channel_id=1, source_target_pairs={{0,32},{32,64},{64,96},{96,128},{128,160},{160,192},{192,224},{1,3... | collective-permute-start | bytes 2752520 | tf_op jit(solution)/shard_map/while/body/eval_jaxpr/ppermute | solution.py:12
  227.8 12.7 %collective-permute-start = (f32[128,1792]{1,0:T(8,128)}, f32[128,1792]{1,0:T(8,128)S(1)}, u32[]{:S(2)}, u32[]{:S(2)}) collective-permute-start(f32[128,1792]{1,0:T(8,128)} %get-tuple-element.455), channel_id=1, source_target_pairs={{0,32},{32,64},{64,96},{96,128},{128,160},{160,192},{192,224},{1,3... | collective-permute-start | bytes 2752520 | tf_op jit(solution)/shard_map/while/body/eval_jaxpr/ppermute | solution.py:12
  240.5 2.2 collective-permute-done
  244.3 12.7 %collective-permute-start = (f32[128,1792]{1,0:T(8,128)}, f32[128,1792]{1,0:T(8,128)S(1)}, u32[]{:S(2)}, u32[]{:S(2)}) collective-permute-start(f32[128,1792]{1,0:T(8,128)} %get-tuple-element.455), channel_id=1, source_target_pairs={{0,32},{32,64},{64,96},{96,128},{128,160},{160,192},{192,224},{1,3... | collective-permute-start | bytes 2752520 | tf_op jit(solution)/shard_map/while/body/eval_jaxpr/ppermute | solution.py:12
  260.7 12.7 %collective-permute-start = (f32[128,1792]{1,0:T(8,128)}, f32[128,1792]{1,0:T(8,128)S(1)}, u32[]{:S(2)}, u32[]{:S(2)}) collective-permute-start(f32[128,1792]{1,0:T(8,128)} %get-tuple-element.455), channel_id=1, source_target_pairs={{0,32},{32,64},{64,96},{96,128},{128,160},{160,192},{192,224},{1,3... | collective-permute-start | bytes 2752520 | tf_op jit(solution)/shard_map/while/body/eval_jaxpr/ppermute | solution.py:12
  276.7 74.4 %all-reduce.2.cloned.1.call-done = f32[128,1792]{1,0:T(8,128)} async-done(((f32[128,1792]{1,0:T(8,128)}), f32[128,1792]{1,0:T(8,128)}) %all-reduce.2.cloned.1.call-update) | async-done | bytes 917520 | tf_op jit(solution)/shard_map/psum | solution.py:47
  351.1 8.4 %fusion.4 = (f32[128,1792]{1,0:T(8,128)S(1)}, f32[128,1792]{1,0:T(8,128)S(1)}, f32[128,1792]{1,0:T(8,128)}) fusion(f32[128,1792]{1,0:T(8,128)} %copy-done, f32[128,1792]{1,0:T(8,128)} %all-reduce.2.cloned.1.call-done, f32[1792]{0:T(1024)S(1)} %get-tuple-element.528, bf16[128,3584]{1,0:T(8,128)(2,1)} %param.8, ...), kind=kOutput, calls=%fused_computation.16 | convolution fusion | flops 1646231552 | bytes 18357248 | tf_op jit(solution)/shard_map/dot_general | solution.py:24
  359.4 99.1 %while.35 = (s32[]{:T(128)}, f32[128,1792]{1,0:T(8,128)}, f32[1792]{0:T(1024)S(1)}, f32[1792]{0:T(1024)S(1)}, f32[128,1792]{1,0:T(8,128)S(1)}, /*index=5*/f32[12...) while((s32[]{:T(128)}, f32[128,1792]{1,0:T(8,128)}, ...), condition=%wide.region_5.6_spmd.clone, body=%wide.region_3.5_spmd.clone.sunk | while | flops 4132359 | bytes 7376058 | solution.py:62
  361.3 2.5 collective-permute-done.1
  368.8 5.9 collective-permute-done.1
  379.8 8.6 %collective-permute-done.1 = bf16[128,1792]{1,0:T(8,128)(2,1)} collective-permute-done((bf16[128,1792]{1,0:T(8,128)(2,1)S(1)}, bf16[128,1792]{1,0:T(8,128)(2,1)}, u32[]{:S(2)}, u32[]{:S(2)}) %collective-permute-start.1) | collective-permute-done | bytes 458784 | tf_op jit(solution)/shard_map/while/body/eval_jaxpr/ppermute | solution.py:12
  393.4 8.6 %collective-permute-done.1 = bf16[128,1792]{1,0:T(8,128)(2,1)} collective-permute-done((bf16[128,1792]{1,0:T(8,128)(2,1)S(1)}, bf16[128,1792]{1,0:T(8,128)(2,1)}, u32[]{:S(2)}, u32[]{:S(2)}) %collective-permute-start.1) | collective-permute-done | bytes 458784 | tf_op jit(solution)/shard_map/while/body/eval_jaxpr/ppermute | solution.py:12
  407.0 8.6 %collective-permute-done.1 = bf16[128,1792]{1,0:T(8,128)(2,1)} collective-permute-done((bf16[128,1792]{1,0:T(8,128)(2,1)S(1)}, bf16[128,1792]{1,0:T(8,128)(2,1)}, u32[]{:S(2)}, u32[]{:S(2)}) %collective-permute-start.1) | collective-permute-done | bytes 458784 | tf_op jit(solution)/shard_map/while/body/eval_jaxpr/ppermute | solution.py:12
  420.7 8.6 %collective-permute-done.1 = bf16[128,1792]{1,0:T(8,128)(2,1)} collective-permute-done((bf16[128,1792]{1,0:T(8,128)(2,1)S(1)}, bf16[128,1792]{1,0:T(8,128)(2,1)}, u32[]{:S(2)}, u32[]{:S(2)}) %collective-permute-start.1) | collective-permute-done | bytes 458784 | tf_op jit(solution)/shard_map/while/body/eval_jaxpr/ppermute | solution.py:12
  434.3 8.6 %collective-permute-done.1 = bf16[128,1792]{1,0:T(8,128)(2,1)} collective-permute-done((bf16[128,1792]{1,0:T(8,128)(2,1)S(1)}, bf16[128,1792]{1,0:T(8,128)(2,1)}, u32[]{:S(2)}, u32[]{:S(2)}) %collective-permute-start.1) | collective-permute-done | bytes 458784 | tf_op jit(solution)/shard_map/while/body/eval_jaxpr/ppermute | solution.py:12
  447.9 8.6 %collective-permute-done.1 = bf16[128,1792]{1,0:T(8,128)(2,1)} collective-permute-done((bf16[128,1792]{1,0:T(8,128)(2,1)S(1)}, bf16[128,1792]{1,0:T(8,128)(2,1)}, u32[]{:S(2)}, u32[]{:S(2)}) %collective-permute-start.1) | collective-permute-done | bytes 458784 | tf_op jit(solution)/shard_map/while/body/eval_jaxpr/ppermute | solution.py:12
  458.5 210.8 %psum.15 = f32[1792]{0:T(1024)} all-reduce(f32[1792]{0:T(1024)S(1)} %get-tuple-element.289), channel_id=1, replica_groups=mesh['tm'=8,'mp'=4,'tok'=8] {'tm','tok'}, use_global_device_ids=true, to_apply=%region_6.7 | all-reduce | flops 1792 | bytes 14336 | tf_op jit(solution)/shard_map/psum | solution.py:65
  (61 shorter events, 68.8 us)
Async XLA Ops:
  7.2 140.9 %all-gather.2.cloned.1.call-start = ((), (), s32[]{:S(2)}) async-start(), calls=%async_computation | async-start | bytes 13045760 | tf_op jit(solution)/shard_map/all_gather | solution.py:22
  7.9 343.2 %all-reduce.2.cloned.1.call-start = ((), (), s32[]{:S(2)}) async-start(), calls=%async_computation.1 | async-start | bytes 1835008 | tf_op jit(solution)/shard_map/psum | solution.py:47
  8.0 147.5 %copy-start.2 = (f32[1792]{0:T(1024)S(1)}, f32[1792]{0:T(1024)}, u32[]{:S(2)}) copy-start(f32[1792]{0:T(1024)} %param.11) | copy-start | bytes 21508
  157.1 4.5 collective-permute-start
  163.1 13.8 %collective-permute-start = (f32[128,1792]{1,0:T(8,128)}, f32[128,1792]{1,0:T(8,128)S(1)}, u32[]{:S(2)}, u32[]{:S(2)}) collective-permute-start(f32[128,1792]{1,0:T(8,128)} %get-tuple-element.455), channel_id=1, source_target_pairs={{0,32},{32,64},{64,96},{96,128},{128,160},{160,192},{192,224},{1,3... | collective-permute-start | bytes 2752520 | tf_op jit(solution)/shard_map/while/body/eval_jaxpr/ppermute | solution.py:12
  178.4 14.9 %collective-permute-start = (f32[128,1792]{1,0:T(8,128)}, f32[128,1792]{1,0:T(8,128)S(1)}, u32[]{:S(2)}, u32[]{:S(2)}) collective-permute-start(f32[128,1792]{1,0:T(8,128)} %get-tuple-element.455), channel_id=1, source_target_pairs={{0,32},{32,64},{64,96},{96,128},{128,160},{160,192},{192,224},{1,3... | collective-permute-start | bytes 2752520 | tf_op jit(solution)/shard_map/while/body/eval_jaxpr/ppermute | solution.py:12
  194.9 14.9 %collective-permute-start = (f32[128,1792]{1,0:T(8,128)}, f32[128,1792]{1,0:T(8,128)S(1)}, u32[]{:S(2)}, u32[]{:S(2)}) collective-permute-start(f32[128,1792]{1,0:T(8,128)} %get-tuple-element.455), channel_id=1, source_target_pairs={{0,32},{32,64},{64,96},{96,128},{128,160},{160,192},{192,224},{1,3... | collective-permute-start | bytes 2752520 | tf_op jit(solution)/shard_map/while/body/eval_jaxpr/ppermute | solution.py:12
  211.4 14.9 %collective-permute-start = (f32[128,1792]{1,0:T(8,128)}, f32[128,1792]{1,0:T(8,128)S(1)}, u32[]{:S(2)}, u32[]{:S(2)}) collective-permute-start(f32[128,1792]{1,0:T(8,128)} %get-tuple-element.455), channel_id=1, source_target_pairs={{0,32},{32,64},{64,96},{96,128},{128,160},{160,192},{192,224},{1,3... | collective-permute-start | bytes 2752520 | tf_op jit(solution)/shard_map/while/body/eval_jaxpr/ppermute | solution.py:12
  227.8 14.9 %collective-permute-start = (f32[128,1792]{1,0:T(8,128)}, f32[128,1792]{1,0:T(8,128)S(1)}, u32[]{:S(2)}, u32[]{:S(2)}) collective-permute-start(f32[128,1792]{1,0:T(8,128)} %get-tuple-element.455), channel_id=1, source_target_pairs={{0,32},{32,64},{64,96},{96,128},{128,160},{160,192},{192,224},{1,3... | collective-permute-start | bytes 2752520 | tf_op jit(solution)/shard_map/while/body/eval_jaxpr/ppermute | solution.py:12
  244.3 14.9 %collective-permute-start = (f32[128,1792]{1,0:T(8,128)}, f32[128,1792]{1,0:T(8,128)S(1)}, u32[]{:S(2)}, u32[]{:S(2)}) collective-permute-start(f32[128,1792]{1,0:T(8,128)} %get-tuple-element.455), channel_id=1, source_target_pairs={{0,32},{32,64},{64,96},{96,128},{128,160},{160,192},{192,224},{1,3... | collective-permute-start | bytes 2752520 | tf_op jit(solution)/shard_map/while/body/eval_jaxpr/ppermute | solution.py:12
  260.7 14.9 %collective-permute-start = (f32[128,1792]{1,0:T(8,128)}, f32[128,1792]{1,0:T(8,128)S(1)}, u32[]{:S(2)}, u32[]{:S(2)}) collective-permute-start(f32[128,1792]{1,0:T(8,128)} %get-tuple-element.455), channel_id=1, source_target_pairs={{0,32},{32,64},{64,96},{96,128},{128,160},{160,192},{192,224},{1,3... | collective-permute-start | bytes 2752520 | tf_op jit(solution)/shard_map/while/body/eval_jaxpr/ppermute | solution.py:12
  275.6 1.0 copy-start
  276.7 82.8 %copy-start.1 = (f32[128,1792]{1,0:T(8,128)S(1)}, f32[128,1792]{1,0:T(8,128)}, u32[]{:S(2)}) copy-start(f32[128,1792]{1,0:T(8,128)} %copy-done) | copy-start | bytes 2752516
  360.0 3.8 collective-permute-start.1
  367.5 7.2 %collective-permute-start.1 = (bf16[128,1792]{1,0:T(8,128)(2,1)S(1)}, bf16[128,1792]{1,0:T(8,128)(2,1)}, u32[]{:S(2)}, u32[]{:S(2)}) collective-permute-start(bf16[128,1792]{1,0:T(8,128)(2,1)S(1)} %get-tuple-element.465), channel_id=1, source_target_pairs={{32,0},{64,32},{96,64},{128,96},{160,128},{192,160},{224,192},{33,... | collective-permute-start | bytes 1376264 | tf_op jit(solution)/shard_map/while/body/eval_jaxpr/ppermute | solution.py:12
  378.5 9.9 %collective-permute-start.1 = (bf16[128,1792]{1,0:T(8,128)(2,1)S(1)}, bf16[128,1792]{1,0:T(8,128)(2,1)}, u32[]{:S(2)}, u32[]{:S(2)}) collective-permute-start(bf16[128,1792]{1,0:T(8,128)(2,1)S(1)} %get-tuple-element.465), channel_id=1, source_target_pairs={{32,0},{64,32},{96,64},{128,96},{160,128},{192,160},{224,192},{33,... | collective-permute-start | bytes 1376264 | tf_op jit(solution)/shard_map/while/body/eval_jaxpr/ppermute | solution.py:12
  392.1 9.9 %collective-permute-start.1 = (bf16[128,1792]{1,0:T(8,128)(2,1)S(1)}, bf16[128,1792]{1,0:T(8,128)(2,1)}, u32[]{:S(2)}, u32[]{:S(2)}) collective-permute-start(bf16[128,1792]{1,0:T(8,128)(2,1)S(1)} %get-tuple-element.465), channel_id=1, source_target_pairs={{32,0},{64,32},{96,64},{128,96},{160,128},{192,160},{224,192},{33,... | collective-permute-start | bytes 1376264 | tf_op jit(solution)/shard_map/while/body/eval_jaxpr/ppermute | solution.py:12
  405.7 9.9 %collective-permute-start.1 = (bf16[128,1792]{1,0:T(8,128)(2,1)S(1)}, bf16[128,1792]{1,0:T(8,128)(2,1)}, u32[]{:S(2)}, u32[]{:S(2)}) collective-permute-start(bf16[128,1792]{1,0:T(8,128)(2,1)S(1)} %get-tuple-element.465), channel_id=1, source_target_pairs={{32,0},{64,32},{96,64},{128,96},{160,128},{192,160},{224,192},{33,... | collective-permute-start | bytes 1376264 | tf_op jit(solution)/shard_map/while/body/eval_jaxpr/ppermute | solution.py:12
  419.3 9.9 %collective-permute-start.1 = (bf16[128,1792]{1,0:T(8,128)(2,1)S(1)}, bf16[128,1792]{1,0:T(8,128)(2,1)}, u32[]{:S(2)}, u32[]{:S(2)}) collective-permute-start(bf16[128,1792]{1,0:T(8,128)(2,1)S(1)} %get-tuple-element.465), channel_id=1, source_target_pairs={{32,0},{64,32},{96,64},{128,96},{160,128},{192,160},{224,192},{33,... | collective-permute-start | bytes 1376264 | tf_op jit(solution)/shard_map/while/body/eval_jaxpr/ppermute | solution.py:12
  433.0 9.9 %collective-permute-start.1 = (bf16[128,1792]{1,0:T(8,128)(2,1)S(1)}, bf16[128,1792]{1,0:T(8,128)(2,1)}, u32[]{:S(2)}, u32[]{:S(2)}) collective-permute-start(bf16[128,1792]{1,0:T(8,128)(2,1)S(1)} %get-tuple-element.465), channel_id=1, source_target_pairs={{32,0},{64,32},{96,64},{128,96},{160,128},{192,160},{224,192},{33,... | collective-permute-start | bytes 1376264 | tf_op jit(solution)/shard_map/while/body/eval_jaxpr/ppermute | solution.py:12
  446.6 9.9 %collective-permute-start.1 = (bf16[128,1792]{1,0:T(8,128)(2,1)S(1)}, bf16[128,1792]{1,0:T(8,128)(2,1)}, u32[]{:S(2)}, u32[]{:S(2)}) collective-permute-start(bf16[128,1792]{1,0:T(8,128)(2,1)S(1)} %get-tuple-element.465), channel_id=1, source_target_pairs={{32,0},{64,32},{96,64},{128,96},{160,128},{192,160},{224,192},{33,... | collective-permute-start | bytes 1376264 | tf_op jit(solution)/shard_map/while/body/eval_jaxpr/ppermute | solution.py:12
Sparse Core Ops, SparseCore 0:
  11.7 136.3 all-gather.1
  276.8 74.2 all-reduce.1
where the time goes:
time: 677 us; the launch traced here: 676 us
  waiting for transfers between devices  293 us (43%)
  blocking collectives  211 us (31%)
  starting transfers between devices  100 us (15%)
  other arithmetic  41 us (6%)
  matrix products  15.7 us (2%)
  between operations  14.1 us (2%)
    psum x1, blocking collectives, on_device(): grad_threshold = lax.psum(grad_local, ('tm', 'tok'))  211 us
    all_gather x1, waiting for transfers between devices, on_device(): piece = lax.all_gather(gate_weight, ('tm', 'tok'), axis=0, tiled=True)  140 us
    ppermute x16, starting transfers between devices, passed_along(): return lax.ppermute(x, axis, pairs)  100 us
    ppermute x16, waiting for transfers between devices, passed_along(): return lax.ppermute(x, axis, pairs)  77.7 us
    psum x1, waiting for transfers between devices, on_device(): total = lax.psum(spikes, 'tm')  74.4 us
    convert_element_type x8, other arithmetic, backward_turn(): passed_along((incoming + dwide).astype(jnp.bfloat16), 'tm', -1)  16.3 us
  transfers between devices with their start and end apart: 18, of which 18 were waited for; matrix products, arithmetic and copies ran while one was open for 0% of the time, Pallas kernels for 0%

commit v1 on v0

--- a/solution.py
+++ b/solution.py
@@ -4,6 +4,14 @@
 from jax.sharding import PartitionSpec as P
 
 SHARP = 2.0
+
+
+def added_up(x, axis):
+    size, summed = (lax.axis_size(axis), x)
+    for far in [1 << k for k in range(size.bit_length() - 1)]:
+        route = [(i, i ^ far) for i in range(size)]
+        summed = summed + lax.ppermute(summed, axis, route)
+    return summed
 
 
 def passed_along(x, axis, by):
@@ -44,7 +52,7 @@
     unused, spikes = lax.fori_loop(
         0, turns, forward_turn, (block_zero, jnp.zeros((rows, width), jnp.float32))
     )
-    total = lax.psum(spikes, "tm")
+    total = added_up(spikes, "tm")
     rates = threshold * total / steps
     error = (rates - target) / tokens_all
 

time: 677 us -> 654 us (0.966)
  waiting for transfers between devices: 293 us -> 257 us
  starting transfers between devices: 100 us -> 117 us
    psum x1 -> x0, waiting for transfers between devices: 74.4 us -> none  [on_device(): total = lax.psum(spikes, 'tm')]
    ppermute x0 -> x3, waiting for transfers between devices: none -> 36.2 us  [added_up(): summed = summed + lax.ppermute(summed, axis, route)]
    ppermute x0 -> x3, starting transfers between devices: none -> 16.8 us  [added_up(): summed = summed + lax.ppermute(summed, axis, route)]
  transfers between devices with their start and end apart: 18 -> 20, of which waited for: 18 -> 20; matrix products, arithmetic and copies ran while one was open for 0% -> 1% of each run, Pallas kernels for 0% -> 0%
where the time goes in v1:
time: 654 us; the launch traced here: 652 us
  waiting for transfers between devices  257 us (39%)
  blocking collectives  205 us (31%)
  starting transfers between devices  117 us (18%)
  other arithmetic  44.1 us (7%)
  matrix products  14.1 us (2%)
  between operations  14.1 us (2%)
    psum x1, blocking collectives, on_device(): grad_threshold = lax.psum(grad_local, ('tm', 'tok'))  205 us
    all_gather x1, waiting for transfers between devices, on_device(): piece = lax.all_gather(gate_weight, ('tm', 'tok'), axis=0, tiled=True)  140 us
    ppermute x16, starting transfers between devices, passed_along(): return lax.ppermute(x, axis, pairs)  100 us
    ppermute x16, waiting for transfers between devices, passed_along(): return lax.ppermute(x, axis, pairs)  79.7 us
    ppermute x3, waiting for transfers between devices, added_up(): summed = summed + lax.ppermute(summed, axis, route)  36.2 us
    ppermute x3, starting transfers between devices, added_up(): summed = summed + lax.ppermute(summed, axis, route)  16.8 us
    convert_element_type x8, other arithmetic, backward_turn(): passed_along((incoming + dwide).astype(jnp.bfloat16), 'tm', -1)  16.5 us
  transfers between devices with their start and end apart: 20, of which 20 were waited for; matrix products, arithmetic and copies ran while one was open for 1% of the time, Pallas kernels for 0%

profile of v1, /device:TPU:32, one launch (start us, length us, event | category | flops | bytes accessed | tf_op | source)
XLA Modules:
  0.0 652.0 jit_solution(9255586875958625832)
XLA Ops:
  7.9 140.1 %all-gather.2.cloned.1.call-done = bf16[3584,1792]{1,0:T(8,128)(2,1)} async-done(((bf16[56,1792]{1,0:T(8,128)(2,1)}), bf16[3584,1792]{1,0:T(8,128)(2,1)}) %all-gather.2.cloned.1.call-update) | async-done | bytes 12845072 | tf_op jit(solution)/shard_map/all_gather | solution.py:30
  148.0 7.4 %convolution_multiply_fusion = f32[128,1792]{1,0:T(8,128)S(1)} fusion(bf16[3584,1792]{1,0:T(8,128)(2,1)} %all-gather.2.cloned.1.call-done, bf16[128,3584]{1,0:T(8,128)(2,1)} %param.8, s32[1,128,3584]{2,1,0:T(8,128)} %param.9), kind=kOutput, calls=%fused_computation.8 | convolution fusion | flops 1645314048 | bytes 16515072 | tf_op jit(solution)/shard_map/dot_general | solution.py:31
  155.5 120.2 %while.34 = (s32[]{:T(128)}, f32[128,1792]{1,0:T(8,128)S(1)}, f32[128,1792]{1,0:T(8,128)S(1)}, f32[128,1792]{1,0:T(8,128)S(1)}, f32[1792]{0:T(1024)S(1)}, /*index=5*/s32[]{:T(128)}, s32[]{:T(128)}, s32[]{:T(128)}) while((s32[]{:T(128)}, f32[128,1792]{1,0:T(8,128)S(1)}, f32[128,1792]{1,0:T(8,128)S(1)}, f32[128,1792]{1,0:T(8,128)S(1)}, ...), condition=%wide.region_1.2_spmd.clone, body=%wide.region_0.1_spmd.clone.sunk | while | flops 2293767 | bytes 8264873 | solution.py:52
  163.1 11.6 %collective-permute-start = (f32[128,1792]{1,0:T(8,128)}, f32[128,1792]{1,0:T(8,128)S(1)}, u32[]{:S(2)}, u32[]{:S(2)}) collective-permute-start(f32[128,1792]{1,0:T(8,128)} %get-tuple-element.455), channel_id=1, source_target_pairs={{0,32},{32,64},{64,96},{96,128},{128,160},{160,192},{192,224},{1,3... | collective-permute-start | bytes 2752520 | tf_op jit(solution)/shard_map/while/body/eval_jaxpr/ppermute | solution.py:20
  178.4 12.7 %collective-permute-start = (f32[128,1792]{1,0:T(8,128)}, f32[128,1792]{1,0:T(8,128)S(1)}, u32[]{:S(2)}, u32[]{:S(2)}) collective-permute-start(f32[128,1792]{1,0:T(8,128)} %get-tuple-element.455), channel_id=1, source_target_pairs={{0,32},{32,64},{64,96},{96,128},{128,160},{160,192},{192,224},{1,3... | collective-permute-start | bytes 2752520 | tf_op jit(solution)/shard_map/while/body/eval_jaxpr/ppermute | solution.py:20
  194.9 12.7 %collective-permute-start = (f32[128,1792]{1,0:T(8,128)}, f32[128,1792]{1,0:T(8,128)S(1)}, u32[]{:S(2)}, u32[]{:S(2)}) collective-permute-start(f32[128,1792]{1,0:T(8,128)} %get-tuple-element.455), channel_id=1, source_target_pairs={{0,32},{32,64},{64,96},{96,128},{128,160},{160,192},{192,224},{1,3... | collective-permute-start | bytes 2752520 | tf_op jit(solution)/shard_map/while/body/eval_jaxpr/ppermute | solution.py:20
  211.4 12.7 %collective-permute-start = (f32[128,1792]{1,0:T(8,128)}, f32[128,1792]{1,0:T(8,128)S(1)}, u32[]{:S(2)}, u32[]{:S(2)}) collective-permute-start(f32[128,1792]{1,0:T(8,128)} %get-tuple-element.455), channel_id=1, source_target_pairs={{0,32},{32,64},{64,96},{96,128},{128,160},{160,192},{192,224},{1,3... | collective-permute-start | bytes 2752520 | tf_op jit(solution)/shard_map/while/body/eval_jaxpr/ppermute | solution.py:20
  227.8 12.7 %collective-permute-start = (f32[128,1792]{1,0:T(8,128)}, f32[128,1792]{1,0:T(8,128)S(1)}, u32[]{:S(2)}, u32[]{:S(2)}) collective-permute-start(f32[128,1792]{1,0:T(8,128)} %get-tuple-element.455), channel_id=1, source_target_pairs={{0,32},{32,64},{64,96},{96,128},{128,160},{160,192},{192,224},{1,3... | collective-permute-start | bytes 2752520 | tf_op jit(solution)/shard_map/while/body/eval_jaxpr/ppermute | solution.py:20
  244.3 12.7 %collective-permute-start = (f32[128,1792]{1,0:T(8,128)}, f32[128,1792]{1,0:T(8,128)S(1)}, u32[]{:S(2)}, u32[]{:S(2)}) collective-permute-start(f32[128,1792]{1,0:T(8,128)} %get-tuple-element.455), channel_id=1, source_target_pairs={{0,32},{32,64},{64,96},{96,128},{128,160},{160,192},{192,224},{1,3... | collective-permute-start | bytes 2752520 | tf_op jit(solution)/shard_map/while/body/eval_jaxpr/ppermute | solution.py:20
  260.7 12.7 %collective-permute-start = (f32[128,1792]{1,0:T(8,128)}, f32[128,1792]{1,0:T(8,128)S(1)}, u32[]{:S(2)}, u32[]{:S(2)}) collective-permute-start(f32[128,1792]{1,0:T(8,128)} %get-tuple-element.455), channel_id=1, source_target_pairs={{0,32},{32,64},{64,96},{96,128},{128,160},{160,192},{192,224},{1,3... | collective-permute-start | bytes 2752520 | tf_op jit(solution)/shard_map/while/body/eval_jaxpr/ppermute | solution.py:20
  275.6 10.7 %collective-permute-start.2 = (f32[128,1792]{1,0:T(8,128)S(1)}, f32[128,1792]{1,0:T(8,128)S(1)}, u32[]{:S(2)}, u32[]{:S(2)}) collective-permute-start(f32[128,1792]{1,0:T(8,128)S(1)} %get-tuple-element.496), channel_id=1, source_target_pairs={{0,32},{32,0},{64,96},{96,64},{128,160},{160,128},{192,224},{224,1... | collective-permute-start | bytes 2752520 | tf_op jit(solution)/shard_map/ppermute | solution.py:13
  291.3 20.7 %collective-permute-done.3 = f32[128,1792]{1,0:T(8,128)S(1)} collective-permute-done((f32[128,1792]{1,0:T(8,128)S(1)}, f32[128,1792]{1,0:T(8,128)S(1)}, u32[]{:S(2)}, u32[]{:S(2)}) %collective-permute-start.3) | collective-permute-done | bytes 917536 | tf_op jit(solution)/shard_map/ppermute | solution.py:13
  312.0 3.4 collective-permute-start.4
  315.4 6.8 %fusion.5 = f32[128,1792]{1,0:T(8,128)S(1)} fusion(bf16[128,3584]{1,0:T(8,128)(2,1)} %param.8, bf16[3584,1792]{1,0:T(8,128)(2,1)} %all-gather.2.cloned.1.call-done), kind=kOutput, calls=%fused_computation.17 | convolution fusion | flops 1644167168 | bytes 14680064 | tf_op jit(solution)/shard_map/dot_general | solution.py:32
  322.2 13.4 %collective-permute-done.4 = f32[128,1792]{1,0:T(8,128)} collective-permute-done((f32[128,1792]{1,0:T(8,128)S(1)}, f32[128,1792]{1,0:T(8,128)}, u32[]{:S(2)}, u32[]{:S(2)}) %collective-permute-start.4) | collective-permute-done | bytes 917536 | tf_op jit(solution)/shard_map/ppermute | solution.py:13
  338.3 101.3 %while.35 = (s32[]{:T(128)}, f32[128,1792]{1,0:T(8,128)}, f32[1792]{0:T(1024)S(1)}, f32[1792]{0:T(1024)S(1)}, f32[128,1792]{1,0:T(8,128)S(1)}, /*index=5*/f32[12...) while((s32[]{:T(128)}, f32[128,1792]{1,0:T(8,128)}, ...), condition=%wide.region_4.5_spmd.clone, body=%wide.region_2.4_spmd.clone.sunk | while | flops 4132359 | bytes 7376066 | solution.py:70
  347.7 7.9 %collective-permute-done.1 = bf16[128,1792]{1,0:T(8,128)(2,1)} collective-permute-done((bf16[128,1792]{1,0:T(8,128)(2,1)S(1)}, bf16[128,1792]{1,0:T(8,128)(2,1)}, u32[]{:S(2)}, u32[]{:S(2)}) %collective-permute-start.1) | collective-permute-done | bytes 458784 | tf_op jit(solution)/shard_map/while/body/eval_jaxpr/ppermute | solution.py:20
  360.7 8.6 %collective-permute-done.1 = bf16[128,1792]{1,0:T(8,128)(2,1)} collective-permute-done((bf16[128,1792]{1,0:T(8,128)(2,1)S(1)}, bf16[128,1792]{1,0:T(8,128)(2,1)}, u32[]{:S(2)}, u32[]{:S(2)}) %collective-permute-start.1) | collective-permute-done | bytes 458784 | tf_op jit(solution)/shard_map/while/body/eval_jaxpr/ppermute | solution.py:20
  374.4 8.6 %collective-permute-done.1 = bf16[128,1792]{1,0:T(8,128)(2,1)} collective-permute-done((bf16[128,1792]{1,0:T(8,128)(2,1)S(1)}, bf16[128,1792]{1,0:T(8,128)(2,1)}, u32[]{:S(2)}, u32[]{:S(2)}) %collective-permute-start.1) | collective-permute-done | bytes 458784 | tf_op jit(solution)/shard_map/while/body/eval_jaxpr/ppermute | solution.py:20
  388.0 8.6 %collective-permute-done.1 = bf16[128,1792]{1,0:T(8,128)(2,1)} collective-permute-done((bf16[128,1792]{1,0:T(8,128)(2,1)S(1)}, bf16[128,1792]{1,0:T(8,128)(2,1)}, u32[]{:S(2)}, u32[]{:S(2)}) %collective-permute-start.1) | collective-permute-done | bytes 458784 | tf_op jit(solution)/shard_map/while/body/eval_jaxpr/ppermute | solution.py:20
  401.7 8.6 %collective-permute-done.1 = bf16[128,1792]{1,0:T(8,128)(2,1)} collective-permute-done((bf16[128,1792]{1,0:T(8,128)(2,1)S(1)}, bf16[128,1792]{1,0:T(8,128)(2,1)}, u32[]{:S(2)}, u32[]{:S(2)}) %collective-permute-start.1) | collective-permute-done | bytes 458784 | tf_op jit(solution)/shard_map/while/body/eval_jaxpr/ppermute | solution.py:20
  415.3 8.6 %collective-permute-done.1 = bf16[128,1792]{1,0:T(8,128)(2,1)} collective-permute-done((bf16[128,1792]{1,0:T(8,128)(2,1)S(1)}, bf16[128,1792]{1,0:T(8,128)(2,1)}, u32[]{:S(2)}, u32[]{:S(2)}) %collective-permute-start.1) | collective-permute-done | bytes 458784 | tf_op jit(solution)/shard_map/while/body/eval_jaxpr/ppermute | solution.py:20
  429.0 8.6 %collective-permute-done.1 = bf16[128,1792]{1,0:T(8,128)(2,1)} collective-permute-done((bf16[128,1792]{1,0:T(8,128)(2,1)S(1)}, bf16[128,1792]{1,0:T(8,128)(2,1)}, u32[]{:S(2)}, u32[]{:S(2)}) %collective-permute-start.1) | collective-permute-done | bytes 458784 | tf_op jit(solution)/shard_map/while/body/eval_jaxpr/ppermute | solution.py:20
  439.6 205.5 %psum.7 = f32[1792]{0:T(1024)} all-reduce(f32[1792]{0:T(1024)S(1)} %get-tuple-element.289), channel_id=1, replica_groups=mesh['tm'=8,'mp'=4,'tok'=8] {'tm','tok'}, use_global_device_ids=true, to_apply=%region_5.6 | all-reduce | flops 1792 | bytes 14336 | tf_op jit(solution)/shard_map/psum | solution.py:73
  (65 shorter events, 82.6 us)
Async XLA Ops:
  7.2 140.9 %all-gather.2.cloned.1.call-start = ((), (), s32[]{:S(2)}) async-start(), calls=%async_computation | async-start | bytes 13045760 | tf_op jit(solution)/shard_map/all_gather | solution.py:30
  7.9 147.6 %copy-start.1 = (f32[1792]{0:T(1024)S(1)}, f32[1792]{0:T(1024)}, u32[]{:S(2)}) copy-start(f32[1792]{0:T(1024)} %param.11) | copy-start | bytes 21508
  157.1 4.5 collective-permute-start
  163.1 13.8 %collective-permute-start = (f32[128,1792]{1,0:T(8,128)}, f32[128,1792]{1,0:T(8,128)S(1)}, u32[]{:S(2)}, u32[]{:S(2)}) collective-permute-start(f32[128,1792]{1,0:T(8,128)} %get-tuple-element.455), channel_id=1, source_target_pairs={{0,32},{32,64},{64,96},{96,128},{128,160},{160,192},{192,224},{1,3... | collective-permute-start | bytes 2752520 | tf_op jit(solution)/shard_map/while/body/eval_jaxpr/ppermute | solution.py:20
  178.4 14.9 %collective-permute-start = (f32[128,1792]{1,0:T(8,128)}, f32[128,1792]{1,0:T(8,128)S(1)}, u32[]{:S(2)}, u32[]{:S(2)}) collective-permute-start(f32[128,1792]{1,0:T(8,128)} %get-tuple-element.455), channel_id=1, source_target_pairs={{0,32},{32,64},{64,96},{96,128},{128,160},{160,192},{192,224},{1,3... | collective-permute-start | bytes 2752520 | tf_op jit(solution)/shard_map/while/body/eval_jaxpr/ppermute | solution.py:20
  194.9 14.9 %collective-permute-start = (f32[128,1792]{1,0:T(8,128)}, f32[128,1792]{1,0:T(8,128)S(1)}, u32[]{:S(2)}, u32[]{:S(2)}) collective-permute-start(f32[128,1792]{1,0:T(8,128)} %get-tuple-element.455), channel_id=1, source_target_pairs={{0,32},{32,64},{64,96},{96,128},{128,160},{160,192},{192,224},{1,3... | collective-permute-start | bytes 2752520 | tf_op jit(solution)/shard_map/while/body/eval_jaxpr/ppermute | solution.py:20
  211.4 14.9 %collective-permute-start = (f32[128,1792]{1,0:T(8,128)}, f32[128,1792]{1,0:T(8,128)S(1)}, u32[]{:S(2)}, u32[]{:S(2)}) collective-permute-start(f32[128,1792]{1,0:T(8,128)} %get-tuple-element.455), channel_id=1, source_target_pairs={{0,32},{32,64},{64,96},{96,128},{128,160},{160,192},{192,224},{1,3... | collective-permute-start | bytes 2752520 | tf_op jit(solution)/shard_map/while/body/eval_jaxpr/ppermute | solution.py:20
  227.8 14.9 %collective-permute-start = (f32[128,1792]{1,0:T(8,128)}, f32[128,1792]{1,0:T(8,128)S(1)}, u32[]{:S(2)}, u32[]{:S(2)}) collective-permute-start(f32[128,1792]{1,0:T(8,128)} %get-tuple-element.455), channel_id=1, source_target_pairs={{0,32},{32,64},{64,96},{96,128},{128,160},{160,192},{192,224},{1,3... | collective-permute-start | bytes 2752520 | tf_op jit(solution)/shard_map/while/body/eval_jaxpr/ppermute | solution.py:20
  244.3 14.9 %collective-permute-start = (f32[128,1792]{1,0:T(8,128)}, f32[128,1792]{1,0:T(8,128)S(1)}, u32[]{:S(2)}, u32[]{:S(2)}) collective-permute-start(f32[128,1792]{1,0:T(8,128)} %get-tuple-element.455), channel_id=1, source_target_pairs={{0,32},{32,64},{64,96},{96,128},{128,160},{160,192},{192,224},{1,3... | collective-permute-start | bytes 2752520 | tf_op jit(solution)/shard_map/while/body/eval_jaxpr/ppermute | solution.py:20
  260.7 14.9 %collective-permute-start = (f32[128,1792]{1,0:T(8,128)}, f32[128,1792]{1,0:T(8,128)S(1)}, u32[]{:S(2)}, u32[]{:S(2)}) collective-permute-start(f32[128,1792]{1,0:T(8,128)} %get-tuple-element.455), channel_id=1, source_target_pairs={{0,32},{32,64},{64,96},{96,128},{128,160},{160,192},{192,224},{1,3... | collective-permute-start | bytes 2752520 | tf_op jit(solution)/shard_map/while/body/eval_jaxpr/ppermute | solution.py:20
  275.6 12.8 %collective-permute-start.2 = (f32[128,1792]{1,0:T(8,128)S(1)}, f32[128,1792]{1,0:T(8,128)S(1)}, u32[]{:S(2)}, u32[]{:S(2)}) collective-permute-start(f32[128,1792]{1,0:T(8,128)S(1)} %get-tuple-element.496), channel_id=1, source_target_pairs={{0,32},{32,0},{64,96},{96,64},{128,160},{160,128},{192,224},{224,1... | collective-permute-start | bytes 2752520 | tf_op jit(solution)/shard_map/ppermute | solution.py:13
  288.6 23.4 %collective-permute-start.3 = (f32[128,1792]{1,0:T(8,128)S(1)}, f32[128,1792]{1,0:T(8,128)S(1)}, u32[]{:S(2)}, u32[]{:S(2)}) collective-permute-start(f32[128,1792]{1,0:T(8,128)S(1)} %add.91), channel_id=1, source_target_pairs={{0,64},{32,96},{64,0},{96,32},{128,192},{160,224},{192,128},{224,1... | collective-permute-start | bytes 2752520 | tf_op jit(solution)/shard_map/ppermute | solution.py:13
  312.0 10.2 %copy-start = (f32[128,1792]{1,0:T(8,128)}, f32[128,1792]{1,0:T(8,128)S(1)}, u32[]{:S(2)}) copy-start(f32[128,1792]{1,0:T(8,128)S(1)} %add.92) | copy-start | bytes 2752516
  312.0 23.6 %collective-permute-start.4 = (f32[128,1792]{1,0:T(8,128)S(1)}, f32[128,1792]{1,0:T(8,128)}, u32[]{:S(2)}, u32[]{:S(2)}) collective-permute-start(f32[128,1792]{1,0:T(8,128)S(1)} %add.92), channel_id=1, source_target_pairs={{0,128},{32,160},{64,192},{96,224},{128,0},{160,32},{192,64},{224,... | collective-permute-start | bytes 2752520 | tf_op jit(solution)/shard_map/ppermute | solution.py:13
  338.8 3.8 collective-permute-start.1
  346.4 9.2 %collective-permute-start.1 = (bf16[128,1792]{1,0:T(8,128)(2,1)S(1)}, bf16[128,1792]{1,0:T(8,128)(2,1)}, u32[]{:S(2)}, u32[]{:S(2)}) collective-permute-start(bf16[128,1792]{1,0:T(8,128)(2,1)S(1)} %get-tuple-element.465), channel_id=1, source_target_pairs={{32,0},{64,32},{96,64},{128,96},{160,128},{192,160},{224,192},{33,... | collective-permute-start | bytes 1376264 | tf_op jit(solution)/shard_map/while/body/eval_jaxpr/ppermute | solution.py:20
  359.4 9.9 %collective-permute-start.1 = (bf16[128,1792]{1,0:T(8,128)(2,1)S(1)}, bf16[128,1792]{1,0:T(8,128)(2,1)}, u32[]{:S(2)}, u32[]{:S(2)}) collective-permute-start(bf16[128,1792]{1,0:T(8,128)(2,1)S(1)} %get-tuple-element.465), channel_id=1, source_target_pairs={{32,0},{64,32},{96,64},{128,96},{160,128},{192,160},{224,192},{33,... | collective-permute-start | bytes 1376264 | tf_op jit(solution)/shard_map/while/body/eval_jaxpr/ppermute | solution.py:20
  373.0 9.9 %collective-permute-start.1 = (bf16[128,1792]{1,0:T(8,128)(2,1)S(1)}, bf16[128,1792]{1,0:T(8,128)(2,1)}, u32[]{:S(2)}, u32[]{:S(2)}) collective-permute-start(bf16[128,1792]{1,0:T(8,128)(2,1)S(1)} %get-tuple-element.465), channel_id=1, source_target_pairs={{32,0},{64,32},{96,64},{128,96},{160,128},{192,160},{224,192},{33,... | collective-permute-start | bytes 1376264 | tf_op jit(solution)/shard_map/while/body/eval_jaxpr/ppermute | solution.py:20
  386.7 9.9 %collective-permute-start.1 = (bf16[128,1792]{1,0:T(8,128)(2,1)S(1)}, bf16[128,1792]{1,0:T(8,128)(2,1)}, u32[]{:S(2)}, u32[]{:S(2)}) collective-permute-start(bf16[128,1792]{1,0:T(8,128)(2,1)S(1)} %get-tuple-element.465), channel_id=1, source_target_pairs={{32,0},{64,32},{96,64},{128,96},{160,128},{192,160},{224,192},{33,... | collective-permute-start | bytes 1376264 | tf_op jit(solution)/shard_map/while/body/eval_jaxpr/ppermute | solution.py:20
  400.4 9.9 %collective-permute-start.1 = (bf16[128,1792]{1,0:T(8,128)(2,1)S(1)}, bf16[128,1792]{1,0:T(8,128)(2,1)}, u32[]{:S(2)}, u32[]{:S(2)}) collective-permute-start(bf16[128,1792]{1,0:T(8,128)(2,1)S(1)} %get-tuple-element.465), channel_id=1, source_target_pairs={{32,0},{64,32},{96,64},{128,96},{160,128},{192,160},{224,192},{33,... | collective-permute-start | bytes 1376264 | tf_op jit(solution)/shard_map/while/body/eval_jaxpr/ppermute | solution.py:20
  414.0 9.9 %collective-permute-start.1 = (bf16[128,1792]{1,0:T(8,128)(2,1)S(1)}, bf16[128,1792]{1,0:T(8,128)(2,1)}, u32[]{:S(2)}, u32[]{:S(2)}) collective-permute-start(bf16[128,1792]{1,0:T(8,128)(2,1)S(1)} %get-tuple-element.465), channel_id=1, source_target_pairs={{32,0},{64,32},{96,64},{128,96},{160,128},{192,160},{224,192},{33,... | collective-permute-start | bytes 1376264 | tf_op jit(solution)/shard_map/while/body/eval_jaxpr/ppermute | solution.py:20
  427.7 9.9 %collective-permute-start.1 = (bf16[128,1792]{1,0:T(8,128)(2,1)S(1)}, bf16[128,1792]{1,0:T(8,128)(2,1)}, u32[]{:S(2)}, u32[]{:S(2)}) collective-permute-start(bf16[128,1792]{1,0:T(8,128)(2,1)S(1)} %get-tuple-element.465), channel_id=1, source_target_pairs={{32,0},{64,32},{96,64},{128,96},{160,128},{192,160},{224,192},{33,... | collective-permute-start | bytes 1376264 | tf_op jit(solution)/shard_map/while/body/eval_jaxpr/ppermute | solution.py:20
Sparse Core Ops, SparseCore 0:
  11.7 136.3 all-gather.1
